TPU v7x, 32 devices: a whole 2x2x4 slice. The times are simulated.
32 devices in a mesh: groups: 2 (over y), depth: 4 (over z), rays: 4 (over x, core).
Axes of the slice: x: 2, y: 2, z: 4, core: 2. Of those that a mesh axis runs over, the one named last changes fastest.
Arguments:
- brick_features: bfloat16 [16, 8, 4, 16384], P(None, ('groups', 'depth'), 'rays'), parts along dimension 1, may hold values from -6 to 6
- entry_cells: int32 [8, 4, 1024], P(('groups', 'depth'), 'rays'), parts along dimension 0, may hold values from 0 to 16368
- sample_counts: int32 [8, 4, 1024], P(('groups', 'depth'), 'rays'), parts along dimension 0, may hold values from 1 to 16, as said below
- brick_rank: int32 [8, 4], P(('groups', 'rays')), parts along dimension 0, may hold values from 0 to 3, each once within a row
- input_layer_weight: bfloat16 [16, 128], replicated, may hold values from -1.5 to 1.5
- second_weight: bfloat16 [128, 33], replicated, may hold values from -0.5 to 0.5
- conv_in: bfloat16 [9, 32, 128], replicated, may hold values from -0.375 to 0.375
- conv_mid: bfloat16 [9, 128, 128], replicated, may hold values from -0.1875 to 0.1875
- conv_out: bfloat16 [9, 128, 128], replicated, may hold values from -0.1875 to 0.1875
Outputs:
- frame: bfloat16 [128, 64, 128], P(('groups', 'depth'), 'rays'), parts along dimension 0
There are 2 independent parts, one for each index of `groups`. A program takes and returns all parts, laid end to end along the dimension named above; an argument that names none is the same for every part. Nothing has to cross between parts.
Inputs may be any that keep to these rules, and one draw needn't show every extreme that they name: `sample_counts`: each brick and strip has a level of at most 16; its rays take 1 to that level samples; some brick and strip reaches 16. `brick_rank`: each row is a permutation of the bricks.
All inputs are finite; a program needn't handle non-finite values.
Results may differ from a plain program's by a relative error of at most 0.015.
Values may be sent and summed in bfloat16 or wider, within the bound.
A program may use at most 64 MiB of HBM per device.

v0:
```python
import math
import jax
import jax.numpy as jnp
from jax import lax
from jax.sharding import PartitionSpec as P

SAMPLES = 16
ROWS_OWN = 16
COLS_DEV = 16


def padded_2(x, sides, width):
    for axis, dim in sides:
        size, length = (lax.axis_size(axis), x.shape[dim])
        up = [(i, (i + 1) % size) for i in range(size - 1)]
        down = [(j, i) for i, j in up]
        last = lax.slice_in_dim(x, length - width, length, axis=dim)
        first = lax.slice_in_dim(x, 0, width, axis=dim)
        before = lax.ppermute(last, axis, up)
        after = lax.ppermute(first, axis, down)
        x = jnp.concatenate([before, x, after], axis=dim)
    return x


def blend_sample_values(field, counts, bricks):
    step_len = 8.0 / (SAMPLES * bricks)
    slot_ids = jnp.arange(SAMPLES, dtype=jnp.int32)
    valid = (slot_ids[:, None] < counts[None, :]).astype(jnp.float32)
    optical = step_len * jax.nn.softplus(field[0]) * valid
    earlier = (slot_ids[:, None] > slot_ids[None, :]).astype(jnp.float32)
    before = jnp.dot(earlier, optical, precision=lax.Precision.HIGHEST)
    weights = jnp.exp(-before) * (1.0 - jnp.exp(-optical))
    colour = jnp.sum(weights[None] * field[1:], axis=1)
    return (colour, jnp.sum(optical, axis=0))


def convolve_valid(padded, weights):
    height = padded.shape[0] - 2
    width = padded.shape[1] - 2
    total = jnp.zeros((height * width, weights.shape[2]), jnp.float32)
    for tap in range(9):
        row_offset_shift, shift_col = divmod(tap, 3)
        window = padded[
            row_offset_shift : row_offset_shift + height, shift_col : shift_col + width
        ].reshape(height * width, -1)
        total = total + jnp.dot(window, weights[tap], preferred_element_type=jnp.float32)
    return total.reshape(height, width, weights.shape[2])


def border_padding(source):
    return padded_2(source, (("depth", 0), ("rays", 1)), 1)


def shards(
    brick_features,
    entry_cells,
    sample_counts,
    brick_rank,
    input_layer_weight,
    second_weight,
    conv_in,
    conv_mid,
    conv_out,
):
    bricks = lax.axis_size("depth")
    feat_count = brick_features.shape[0]
    cell_count = brick_features.shape[3]
    windows = cell_count // SAMPLES
    span = SAMPLES * feat_count
    table = (
        brick_features.reshape(feat_count, windows, SAMPLES)
        .transpose(1, 2, 0)
        .reshape(windows, span)
    )
    entries = entry_cells.reshape(-1)
    counts = sample_counts.reshape(-1)
    ranks = brick_rank.reshape(-1)
    total_rays = entries.shape[0]
    block = math.gcd(total_rays, 512)
    shift_bits = (SAMPLES - 1).bit_length()

    def march_block(operands):
        block_entries, block_counts = operands
        window_ids = block_entries // SAMPLES
        offset = block_entries - window_ids * SAMPLES
        following = jnp.minimum(window_ids + 1, windows - 1)
        paired = jnp.concatenate(
            [jnp.take(table, window_ids, axis=0), jnp.take(table, following, axis=0)], axis=1
        )
        for level in range(shift_bits):
            moved_by = (1 << level) * feat_count
            moved = jnp.concatenate(
                [paired[:, moved_by:], jnp.zeros((block, moved_by), paired.dtype)], axis=1
            )
            taken = (offset >> level & 1)[:, None] == 1
            paired = jnp.where(taken, moved, paired)
        probed_values = paired[:, :span].reshape(block, SAMPLES, feat_count)
        before_activation = jnp.einsum(
            "fh,isf->hsi", input_layer_weight, probed_values, preferred_element_type=jnp.float32
        )
        hidden = (
            jnp.maximum(before_activation, 0.0).astype(jnp.bfloat16).reshape(-1, SAMPLES * block)
        )
        field = jnp.einsum("ho,hn->on", second_weight, hidden, preferred_element_type=jnp.float32)
        return blend_sample_values(field.reshape(-1, SAMPLES, block), block_counts, bricks)

    colour_blocks, depth_blocks = lax.map(
        march_block, (entries.reshape(-1, block), counts.reshape(-1, block))
    )
    colour = jnp.transpose(colour_blocks, (1, 0, 2)).reshape(colour_blocks.shape[1], total_rays)
    depth_sum = depth_blocks.reshape(1, total_rays)
    all_depth = lax.all_gather(depth_sum, "depth", axis=0, tiled=True)
    my_rank = ranks[lax.axis_index("depth")]
    ahead = (ranks < my_rank).astype(jnp.float32)[None, :]
    front = jnp.dot(ahead, all_depth, precision=lax.Precision.HIGHEST)
    image = lax.psum_scatter(
        (colour * jnp.exp(-front)).astype(jnp.bfloat16), "depth", scatter_dimension=1, tiled=True
    ).astype(jnp.float32)
    image = image.reshape(-1, ROWS_OWN, COLS_DEV).transpose(1, 2, 0).astype(jnp.bfloat16)
    first = jnp.maximum(convolve_valid(border_padding(image), conv_in), 0.0).astype(jnp.bfloat16)
    second = jnp.maximum(convolve_valid(border_padding(first), conv_mid), 0.0).astype(jnp.bfloat16)
    frame = convolve_valid(border_padding(second), conv_out).astype(jnp.bfloat16)
    return frame


def solution(mesh):
    placed = (
        P(None, ("groups", "depth"), "rays", None),
        P(("groups", "depth"), "rays", None),
        P(("groups", "depth"), "rays", None),
        P(("groups", "rays"), None),
        P(),
        P(),
        P(),
        P(),
        P(),
    )
    return jax.shard_map(
        shards,
        mesh=mesh,
        in_specs=placed,
        out_specs=P(("groups", "depth"), "rays", None),
        check_vma=False,
    )
```

profile of v0, /device:TPU:1, one launch (start us, length us, event | category | flops | bytes accessed | tf_op | source)
XLA Modules:
  0.0 133.9 jit_solution(3947614905401499600)
XLA Ops:
  9.6 5.4 %reshape.274 = bf16[16,1024,16]{2,1,0:T(8,128)(2,1)} reshape(bf16[16,1,1,16384]{3,0,2,1:T(8,128)(2,1)} %param.13) | data formatting | bytes 1048576 | tf_op jit(solution)/shard_map/reshape | solution.py:71
  15.1 3.7 %copy.18 = bf16[1024,16,16]{0,2,1:T(8,128)(2,1)S(1)} copy(bf16[1024,16,16]{1,0,2:T(8,128)(2,1)} %bitcast.218) | data formatting | bytes 1048576 | tf_op jit(solution)/shard_map/transpose | solution.py:72
  19.0 19.6 %while.14 = (s32[]{:T(128)}, f32[2,32,512]{2,1,0:T(8,128)S(1)}, f32[2,512]{1,0:T(2,128)S(1)}, s32[2,512]{1,0:T(2,128)S(1)}, s32[2,512]{1,0:T(2,128)S(1)}, /*inde...) while((s32[]{:T(128)}, f32[2,32,512]{2,1,0:T(8,128)S(1)}, ...), condition=%wide.region_3.5_spmd, body=%wide.region_0.4_spmd.sunk | while | flops 110472448 | bytes 23171440 | solution.py:107
  19.1 2.0 %gather_fusion.1 = bf16[512,256]{1,0:T(8,128)(2,1)S(1)} fusion(bf16[1024,256]{1,0:T(8,128)(2,1)S(1)} %get-tuple-element.298, s32[1024]{0:T(1024)S(1)} %pad_clamp_fusion.5), kind=kCustom, calls=%fused_computation.clone.clone.1 | custom fusion | bytes 526336 | tf_op jit(solution)/shard_map/while/body/eval_jaxpr/jit(_take)/gather | solution.py:88
  21.2 2.0 %gather_fusion = bf16[512,256]{1,0:T(8,128)(2,1)S(1)} fusion(bf16[1024,256]{1,0:T(8,128)(2,1)S(1)} %get-tuple-element.298, s32[1024]{0:T(1024)S(1)} %pad_clamp_fusion.4), kind=kCustom, calls=%fused_computation.1.clone.clone.1 | custom fusion | bytes 526336 | tf_op jit(solution)/shard_map/while/body/eval_jaxpr/jit(_take)/gather | solution.py:88
  26.1 1.3 convolution_bitcast_fusion.2
  28.9 2.0 %gather_fusion.1 = bf16[512,256]{1,0:T(8,128)(2,1)S(1)} fusion(bf16[1024,256]{1,0:T(8,128)(2,1)S(1)} %get-tuple-element.298, s32[1024]{0:T(1024)S(1)} %pad_clamp_fusion.5), kind=kCustom, calls=%fused_computation.clone.clone.1 | custom fusion | bytes 526336 | tf_op jit(solution)/shard_map/while/body/eval_jaxpr/jit(_take)/gather | solution.py:88
  31.0 2.0 %gather_fusion = bf16[512,256]{1,0:T(8,128)(2,1)S(1)} fusion(bf16[1024,256]{1,0:T(8,128)(2,1)S(1)} %get-tuple-element.298, s32[1024]{0:T(1024)S(1)} %pad_clamp_fusion.4), kind=kCustom, calls=%fused_computation.1.clone.clone.1 | custom fusion | bytes 526336 | tf_op jit(solution)/shard_map/while/body/eval_jaxpr/jit(_take)/gather | solution.py:88
  38.6 11.3 %all-gather = f32[4,1,1024]{2,1,0:T(1,128)S(1)} all-gather(f32[1,1,1024]{2,1,0:T(1,128)S(1)} %reshape.322), channel_id=1, replica_groups=mesh['groups'=2,'depth'=4,'rays'=4] {'depth'}, dimensions={0}, use_global_device_ids=true | all-gather | bytes 20480 | tf_op jit(solution)/shard_map/all_gather | solution.py:112
  52.0 20.8 %reduce-scatter.2.cloned.1.call-done = bf16[32,256]{1,0:T(8,128)(2,1)} async-done(((bf16[32,1024]{1,0:T(8,128)(2,1)}), bf16[32,256]{1,0:T(8,128)(2,1)}) %reduce-scatter.2.cloned.1.call-update) | async-done | bytes 16400 | tf_op jit(solution)/shard_map/reduce_scatter | solution.py:116
  76.2 3.0 %collective-permute-done.1 = bf16[1,16,32]{2,1,0:T(8,128)(2,1)S(1)} collective-permute-done((bf16[1,16,32]{2,1,0:T(8,128)(2,1)S(1)}, bf16[1,16,32]{2,1,0:T(8,128)(2,1)S(1)}, u32[]{:S(2)}, u32[]{:S(2)}) %collective-permute-start.1) | collective-permute-done | bytes 1056 | tf_op jit(solution)/shard_map/ppermute | solution.py:20
  79.3 7.1 %collective-permute-start.2 = (bf16[18,1,32]{2,1,0:T(2,128)(2,1)S(1)}, bf16[18,1,32]{2,1,0:T(2,128)(2,1)S(1)}, u32[]{:S(2)}, u32[]{:S(2)}) collective-permute-start(bf16[18,1,32]{2,1,0:T(2,128)(2,1)S(1)} %get-tuple-element.183), channel_id=1, source_target_pairs={{0,1},{1,2},{2,3},{4,5},{5,6},{6,7},{8,9},{9,10},{10,11},{12,13},{... | collective-permute-start | bytes 3464 | tf_op jit(solution)/shard_map/ppermute | solution.py:19
  86.4 1.9 %collective-permute-start.3 = (bf16[18,1,32]{2,1,0:T(2,128)(2,1)S(1)}, bf16[18,1,32]{2,1,0:T(2,128)(2,1)S(1)}, u32[]{:S(2)}, u32[]{:S(2)}) collective-permute-start(bf16[18,1,32]{2,1,0:T(2,128)(2,1)S(1)} %get-tuple-element.184), channel_id=1, source_target_pairs={{1,0},{2,1},{3,2},{5,4},{6,5},{7,6},{9,8},{10,9},{11,10},{13,12},{... | collective-permute-start | bytes 3464 | tf_op jit(solution)/shard_map/ppermute | solution.py:20
  88.5 2.9 %collective-permute-done.3 = bf16[18,1,32]{2,1,0:T(2,128)(2,1)S(1)} collective-permute-done((bf16[18,1,32]{2,1,0:T(2,128)(2,1)S(1)}, bf16[18,1,32]{2,1,0:T(2,128)(2,1)S(1)}, u32[]{:S(2)}, u32[]{:S(2)}) %collective-permute-start.3) | collective-permute-done | bytes 1184 | tf_op jit(solution)/shard_map/ppermute | solution.py:20
  92.7 3.4 %collective-permute-start.4 = (bf16[1,16,128]{2,1,0:T(8,128)(2,1)S(1)}, bf16[1,16,128]{2,1,0:T(8,128)(2,1)S(1)}, u32[]{:S(2)}, u32[]{:S(2)}) collective-permute-start(bf16[1,16,128]{2,1,0:T(8,128)(2,1)S(1)} %get-tuple-element.191), channel_id=1, source_target_pairs={{0,4},{4,8},{8,12},{1,5},{5,9},{9,13},{2,6},{6,10},{10,14},{3,7},{... | collective-permute-start | bytes 12296 | tf_op jit(solution)/shard_map/ppermute | solution.py:19
  97.4 3.0 %collective-permute-done.5 = bf16[1,16,128]{2,1,0:T(8,128)(2,1)S(1)} collective-permute-done((bf16[1,16,128]{2,1,0:T(8,128)(2,1)S(1)}, bf16[1,16,128]{2,1,0:T(8,128)(2,1)S(1)}, u32[]{:S(2)}, u32[]{:S(2)}) %collective-permute-start.5) | collective-permute-done | bytes 4128 | tf_op jit(solution)/shard_map/ppermute | solution.py:20
  100.4 3.4 %collective-permute-start.6 = (bf16[18,1,128]{2,1,0:T(2,128)(2,1)S(1)}, bf16[18,1,128]{2,1,0:T(2,128)(2,1)S(1)}, u32[]{:S(2)}, u32[]{:S(2)}) collective-permute-start(bf16[18,1,128]{2,1,0:T(2,128)(2,1)S(1)} %get-tuple-element.179), channel_id=1, source_target_pairs={{0,1},{1,2},{2,3},{4,5},{5,6},{6,7},{8,9},{9,10},{10,11},{12,13},{... | collective-permute-start | bytes 13832 | tf_op jit(solution)/shard_map/ppermute | solution.py:19
  103.8 1.9 %collective-permute-start.7 = (bf16[18,1,128]{2,1,0:T(2,128)(2,1)S(1)}, bf16[18,1,128]{2,1,0:T(2,128)(2,1)S(1)}, u32[]{:S(2)}, u32[]{:S(2)}) collective-permute-start(bf16[18,1,128]{2,1,0:T(2,128)(2,1)S(1)} %get-tuple-element.180), channel_id=1, source_target_pairs={{1,0},{2,1},{3,2},{5,4},{6,5},{7,6},{9,8},{10,9},{11,10},{13,12},{... | collective-permute-start | bytes 13832 | tf_op jit(solution)/shard_map/ppermute | solution.py:20
  106.0 2.9 %collective-permute-done.7 = bf16[18,1,128]{2,1,0:T(2,128)(2,1)S(1)} collective-permute-done((bf16[18,1,128]{2,1,0:T(2,128)(2,1)S(1)}, bf16[18,1,128]{2,1,0:T(2,128)(2,1)S(1)}, u32[]{:S(2)}, u32[]{:S(2)}) %collective-permute-start.7) | collective-permute-done | bytes 4640 | tf_op jit(solution)/shard_map/ppermute | solution.py:20
  110.2 2.1 %collective-permute-start.8 = (bf16[1,16,128]{2,1,0:T(8,128)(2,1)S(1)}, bf16[1,16,128]{2,1,0:T(8,128)(2,1)S(1)}, u32[]{:S(2)}, u32[]{:S(2)}) collective-permute-start(bf16[1,16,128]{2,1,0:T(8,128)(2,1)S(1)} %get-tuple-element.187), channel_id=1, source_target_pairs={{0,4},{4,8},{8,12},{1,5},{5,9},{9,13},{2,6},{6,10},{10,14},{3,7},{... | collective-permute-start | bytes 12296 | tf_op jit(solution)/shard_map/ppermute | solution.py:19
  113.6 3.0 %collective-permute-done.9 = bf16[1,16,128]{2,1,0:T(8,128)(2,1)S(1)} collective-permute-done((bf16[1,16,128]{2,1,0:T(8,128)(2,1)S(1)}, bf16[1,16,128]{2,1,0:T(8,128)(2,1)S(1)}, u32[]{:S(2)}, u32[]{:S(2)}) %collective-permute-start.9) | collective-permute-done | bytes 4128 | tf_op jit(solution)/shard_map/ppermute | solution.py:20
  116.7 3.4 %collective-permute-start.10 = (bf16[18,1,128]{2,1,0:T(2,128)(2,1)S(1)}, bf16[18,1,128]{2,1,0:T(2,128)(2,1)S(1)}, u32[]{:S(2)}, u32[]{:S(2)}) collective-permute-start(bf16[18,1,128]{2,1,0:T(2,128)(2,1)S(1)} %get-tuple-element.175), channel_id=1, source_target_pairs={{0,1},{1,2},{2,3},{4,5},{5,6},{6,7},{8,9},{9,10},{10,11},{12,13},{... | collective-permute-start | bytes 13832 | tf_op jit(solution)/shard_map/ppermute | solution.py:19
  120.1 1.9 %collective-permute-start.11 = (bf16[18,1,128]{2,1,0:T(2,128)(2,1)S(1)}, bf16[18,1,128]{2,1,0:T(2,128)(2,1)S(1)}, u32[]{:S(2)}, u32[]{:S(2)}) collective-permute-start(bf16[18,1,128]{2,1,0:T(2,128)(2,1)S(1)} %get-tuple-element.176), channel_id=1, source_target_pairs={{1,0},{2,1},{3,2},{5,4},{6,5},{7,6},{9,8},{10,9},{11,10},{13,12},{... | collective-permute-start | bytes 13832 | tf_op jit(solution)/shard_map/ppermute | solution.py:20
  122.2 2.9 %collective-permute-done.11 = bf16[18,1,128]{2,1,0:T(2,128)(2,1)S(1)} collective-permute-done((bf16[18,1,128]{2,1,0:T(2,128)(2,1)S(1)}, bf16[18,1,128]{2,1,0:T(2,128)(2,1)S(1)}, u32[]{:S(2)}, u32[]{:S(2)}) %collective-permute-start.11) | collective-permute-done | bytes 4640 | tf_op jit(solution)/shard_map/ppermute | solution.py:20
  (140 shorter events, 26.4 us)
Async XLA Ops:
  6.5 66.3 %reduce-scatter.2.cloned.1.call-start = ((), (), s32[]{:S(2)}) async-start(), calls=%async_computation.1 | async-start | bytes 81920 | tf_op jit(solution)/shard_map/reduce_scatter | solution.py:116
  15.1 3.9 %copy-start.2 = (bf16[128,33]{0,1:T(8,128)(2,1)S(1)}, bf16[128,33]{0,1:T(8,128)(2,1)}, u32[]{:S(2)}) copy-start(bf16[128,33]{0,1:T(8,128)(2,1)} %param.18) | copy-start | bytes 25348
  15.1 3.9 %copy-start.3 = (bf16[16,128]{1,0:T(8,128)(2,1)S(1)}, bf16[16,128]{1,0:T(8,128)(2,1)}, u32[]{:S(2)}) copy-start(bf16[16,128]{1,0:T(8,128)(2,1)} %param.17) | copy-start | bytes 12292
  19.0 30.9 %copy-start.5 = (s32[1,4]{1,0:T(1,128)S(1)}, s32[1,4]{1,0:T(1,128)}, u32[]{:S(2)}) copy-start(s32[1,4]{1,0:T(1,128)} %param.16) | copy-start | bytes 52
  19.0 69.4 %copy-start.4 = (bf16[9,32,128]{2,1,0:T(8,128)(2,1)S(1)}, bf16[9,32,128]{2,1,0:T(8,128)(2,1)}, u32[]{:S(2)}) copy-start(bf16[9,32,128]{2,1,0:T(8,128)(2,1)} %param.19) | copy-start | bytes 221188
  73.6 2.6 %collective-permute-start = (bf16[1,16,32]{2,1,0:T(8,128)(2,1)S(1)}, bf16[1,16,32]{2,1,0:T(8,128)(2,1)S(1)}, u32[]{:S(2)}, u32[]{:S(2)}) collective-permute-start(bf16[1,16,32]{2,1,0:T(8,128)(2,1)S(1)} %get-tuple-element.195), channel_id=1, source_target_pairs={{0,4},{4,8},{8,12},{1,5},{5,9},{9,13},{2,6},{6,10},{10,14},{3,7},{... | collective-permute-start | bytes 3080 | tf_op jit(solution)/shard_map/ppermute | solution.py:19
  74.9 4.4 %collective-permute-start.1 = (bf16[1,16,32]{2,1,0:T(8,128)(2,1)S(1)}, bf16[1,16,32]{2,1,0:T(8,128)(2,1)S(1)}, u32[]{:S(2)}, u32[]{:S(2)}) collective-permute-start(bf16[1,16,32]{2,1,0:T(8,128)(2,1)S(1)} %get-tuple-element.196), channel_id=1, source_target_pairs={{4,0},{8,4},{12,8},{5,1},{9,5},{13,9},{6,2},{10,6},{14,10},{7,3},{... | collective-permute-start | bytes 3080 | tf_op jit(solution)/shard_map/ppermute | solution.py:20
  79.3 9.2 %collective-permute-start.2 = (bf16[18,1,32]{2,1,0:T(2,128)(2,1)S(1)}, bf16[18,1,32]{2,1,0:T(2,128)(2,1)S(1)}, u32[]{:S(2)}, u32[]{:S(2)}) collective-permute-start(bf16[18,1,32]{2,1,0:T(2,128)(2,1)S(1)} %get-tuple-element.183), channel_id=1, source_target_pairs={{0,1},{1,2},{2,3},{4,5},{5,6},{6,7},{8,9},{9,10},{10,11},{12,13},{... | collective-permute-start | bytes 3464 | tf_op jit(solution)/shard_map/ppermute | solution.py:19
  86.4 5.0 %collective-permute-start.3 = (bf16[18,1,32]{2,1,0:T(2,128)(2,1)S(1)}, bf16[18,1,32]{2,1,0:T(2,128)(2,1)S(1)}, u32[]{:S(2)}, u32[]{:S(2)}) collective-permute-start(bf16[18,1,32]{2,1,0:T(2,128)(2,1)S(1)} %get-tuple-element.184), channel_id=1, source_target_pairs={{1,0},{2,1},{3,2},{5,4},{6,5},{7,6},{9,8},{10,9},{11,10},{13,12},{... | collective-permute-start | bytes 3464 | tf_op jit(solution)/shard_map/ppermute | solution.py:20
  88.4 17.4 %copy-start = (bf16[9,128,128]{2,1,0:T(8,128)(2,1)S(1)}, bf16[9,128,128]{2,1,0:T(8,128)(2,1)}, u32[]{:S(2)}) copy-start(bf16[9,128,128]{2,1,0:T(8,128)(2,1)} %param.20) | copy-start | bytes 884740
  92.7 4.7 %collective-permute-start.4 = (bf16[1,16,128]{2,1,0:T(8,128)(2,1)S(1)}, bf16[1,16,128]{2,1,0:T(8,128)(2,1)S(1)}, u32[]{:S(2)}, u32[]{:S(2)}) collective-permute-start(bf16[1,16,128]{2,1,0:T(8,128)(2,1)S(1)} %get-tuple-element.191), channel_id=1, source_target_pairs={{0,4},{4,8},{8,12},{1,5},{5,9},{9,13},{2,6},{6,10},{10,14},{3,7},{... | collective-permute-start | bytes 12296 | tf_op jit(solution)/shard_map/ppermute | solution.py:19
  96.1 4.4 %collective-permute-start.5 = (bf16[1,16,128]{2,1,0:T(8,128)(2,1)S(1)}, bf16[1,16,128]{2,1,0:T(8,128)(2,1)S(1)}, u32[]{:S(2)}, u32[]{:S(2)}) collective-permute-start(bf16[1,16,128]{2,1,0:T(8,128)(2,1)S(1)} %get-tuple-element.192), channel_id=1, source_target_pairs={{4,0},{8,4},{12,8},{5,1},{9,5},{13,9},{6,2},{10,6},{14,10},{7,3},{... | collective-permute-start | bytes 12296 | tf_op jit(solution)/shard_map/ppermute | solution.py:20
  100.4 5.5 %collective-permute-start.6 = (bf16[18,1,128]{2,1,0:T(2,128)(2,1)S(1)}, bf16[18,1,128]{2,1,0:T(2,128)(2,1)S(1)}, u32[]{:S(2)}, u32[]{:S(2)}) collective-permute-start(bf16[18,1,128]{2,1,0:T(2,128)(2,1)S(1)} %get-tuple-element.179), channel_id=1, source_target_pairs={{0,1},{1,2},{2,3},{4,5},{5,6},{6,7},{8,9},{9,10},{10,11},{12,13},{... | collective-permute-start | bytes 13832 | tf_op jit(solution)/shard_map/ppermute | solution.py:19
  103.8 5.0 %collective-permute-start.7 = (bf16[18,1,128]{2,1,0:T(2,128)(2,1)S(1)}, bf16[18,1,128]{2,1,0:T(2,128)(2,1)S(1)}, u32[]{:S(2)}, u32[]{:S(2)}) collective-permute-start(bf16[18,1,128]{2,1,0:T(2,128)(2,1)S(1)} %get-tuple-element.180), channel_id=1, source_target_pairs={{1,0},{2,1},{3,2},{5,4},{6,5},{7,6},{9,8},{10,9},{11,10},{13,12},{... | collective-permute-start | bytes 13832 | tf_op jit(solution)/shard_map/ppermute | solution.py:20
  105.9 16.1 %copy-start.1 = (bf16[9,128,128]{2,1,0:T(8,128)(2,1)S(1)}, bf16[9,128,128]{2,1,0:T(8,128)(2,1)}, u32[]{:S(2)}) copy-start(bf16[9,128,128]{2,1,0:T(8,128)(2,1)} %param.21) | copy-start | bytes 884740
  110.2 3.5 %collective-permute-start.8 = (bf16[1,16,128]{2,1,0:T(8,128)(2,1)S(1)}, bf16[1,16,128]{2,1,0:T(8,128)(2,1)S(1)}, u32[]{:S(2)}, u32[]{:S(2)}) collective-permute-start(bf16[1,16,128]{2,1,0:T(8,128)(2,1)S(1)} %get-tuple-element.187), channel_id=1, source_target_pairs={{0,4},{4,8},{8,12},{1,5},{5,9},{9,13},{2,6},{6,10},{10,14},{3,7},{... | collective-permute-start | bytes 12296 | tf_op jit(solution)/shard_map/ppermute | solution.py:19
  112.3 4.4 %collective-permute-start.9 = (bf16[1,16,128]{2,1,0:T(8,128)(2,1)S(1)}, bf16[1,16,128]{2,1,0:T(8,128)(2,1)S(1)}, u32[]{:S(2)}, u32[]{:S(2)}) collective-permute-start(bf16[1,16,128]{2,1,0:T(8,128)(2,1)S(1)} %get-tuple-element.188), channel_id=1, source_target_pairs={{4,0},{8,4},{12,8},{5,1},{9,5},{13,9},{6,2},{10,6},{14,10},{7,3},{... | collective-permute-start | bytes 12296 | tf_op jit(solution)/shard_map/ppermute | solution.py:20
  116.7 5.5 %collective-permute-start.10 = (bf16[18,1,128]{2,1,0:T(2,128)(2,1)S(1)}, bf16[18,1,128]{2,1,0:T(2,128)(2,1)S(1)}, u32[]{:S(2)}, u32[]{:S(2)}) collective-permute-start(bf16[18,1,128]{2,1,0:T(2,128)(2,1)S(1)} %get-tuple-element.175), channel_id=1, source_target_pairs={{0,1},{1,2},{2,3},{4,5},{5,6},{6,7},{8,9},{9,10},{10,11},{12,13},{... | collective-permute-start | bytes 13832 | tf_op jit(solution)/shard_map/ppermute | solution.py:19
  120.1 5.0 %collective-permute-start.11 = (bf16[18,1,128]{2,1,0:T(2,128)(2,1)S(1)}, bf16[18,1,128]{2,1,0:T(2,128)(2,1)S(1)}, u32[]{:S(2)}, u32[]{:S(2)}) collective-permute-start(bf16[18,1,128]{2,1,0:T(2,128)(2,1)S(1)} %get-tuple-element.176), channel_id=1, source_target_pairs={{1,0},{2,1},{3,2},{5,4},{6,5},{7,6},{9,8},{10,9},{11,10},{13,12},{... | collective-permute-start | bytes 13832 | tf_op jit(solution)/shard_map/ppermute | solution.py:20
Sparse Core Ops, SparseCore 0:
  52.1 20.6 reduce-scatter.1
where the time goes:
time: 135 us; the launch traced here: 134 us
  waiting for transfers between devices  38.6 us (29%)
  starting transfers between devices  30.3 us (22%)
  local copies, waits for them, and re-layouts  22.4 us (17%)
  between operations  13.9 us (10%)
  blocking collectives  11.3 us (8%)
  matrix products  9.79 us (7%)
  other arithmetic  7.22 us (5%)
    reduce_scatter x1, waiting for transfers between devices, shards(): lax.psum_scatter((colour * jnp.exp(-front)).astype(jnp.bfloat16), 'depth'...  20.8 us
    ppermute x6, starting transfers between devices, padded_2(): before = lax.ppermute(last, axis, up)  20.7 us
    ppermute x6, waiting for transfers between devices, padded_2(): after = lax.ppermute(first, axis, down)  17.7 us
    all_gather x1, blocking collectives, shards(): all_depth = lax.all_gather(depth_sum, 'depth', axis=0, tiled=True)  11.3 us
    ppermute x6, starting transfers between devices, padded_2(): after = lax.ppermute(first, axis, down)  9.64 us
    reshape x1, local copies, waits for them, and re-layouts, shards(): brick_features.reshape(feat_count, windows, SAMPLES).transpose(1, 2, 0)  5.43 us
    dot_general x27, matrix products, convolve_valid(): jnp.dot(window, weights[tap], preferred_element_type=jnp.float32)  4.52 us
    gather x2, local copies, waits for them, and re-layouts, march_block(): jnp.take(table, following, axis=0)  3.91 us
  transfers between devices with their start and end apart: 13, of which 7 were waited for; matrix products, arithmetic and copies ran while one was open for 0% of the time, Pallas kernels for 0%

commit v1 on v0

--- a/solution.py
+++ b/solution.py
@@ -7,6 +7,27 @@
 SAMPLES = 16
 ROWS_OWN = 16
 COLS_DEV = 16
+
+
+def collect(shard, axis, dim):
+    size, index, rows = (lax.axis_size(axis), lax.axis_index(axis), shard.shape[dim])
+    right = [(i, (i + 1) % size) for i in range(size)]
+    left = [(i, (i - 1) % size) for i in range(size)]
+    result = jnp.zeros((*shard.shape[:dim], size * rows, *shard.shape[dim + 1 :]), shard.dtype)
+    result = lax.dynamic_update_slice_in_dim(result, shard, index * rows, axis=dim)
+    from_left = from_right = shard
+    half = size // 2
+    for step in range(1, half + 1):
+        from_left = lax.ppermute(from_left, axis, right)
+        result = lax.dynamic_update_slice_in_dim(
+            result, from_left, (index - step) % size * rows, axis=dim
+        )
+        if step < size - half:
+            from_right = lax.ppermute(from_right, axis, left)
+            result = lax.dynamic_update_slice_in_dim(
+                result, from_right, (index + step) % size * rows, axis=dim
+            )
+    return result
 
 
 def padded_2(x, sides, width):
@@ -109,7 +130,7 @@
     )
     colour = jnp.transpose(colour_blocks, (1, 0, 2)).reshape(colour_blocks.shape[1], total_rays)
     depth_sum = depth_blocks.reshape(1, total_rays)
-    all_depth = lax.all_gather(depth_sum, "depth", axis=0, tiled=True)
+    all_depth = collect(depth_sum, "depth", 0)
     my_rank = ranks[lax.axis_index("depth")]
     ahead = (ranks < my_rank).astype(jnp.float32)[None, :]
     front = jnp.dot(ahead, all_depth, precision=lax.Precision.HIGHEST)

time: 135 us -> 129 us (0.956)
  blocking collectives: 11.3 us -> 0 us
  starting transfers between devices: 30.3 us -> 37.1 us
  waiting for transfers between devices: 38.6 us -> 37.1 us
    all_gather x1 -> x0, blocking collectives: 11.3 us -> none  [shards(): all_depth = lax.all_gather(depth_sum, 'depth', axis=0, tiled=True)]
    ppermute x0 -> x3, waiting for transfers between devices: none -> 4.32 us  [the longest x2 4.32 us: collect(): from_left = lax.ppermute(from_left, axis, right)]
    ppermute x0 -> x3, starting transfers between devices: none -> 4.27 us  [the longest x2 2.19 us: collect(): from_left = lax.ppermute(from_left, axis, right)]
    reduce_scatter x1, waiting for transfers between devices: 20.8 us -> 17.4 us  [shards(): lax.psum_scatter((colour * jnp.exp(-front)).astype(jnp.bfloat16), 'depth'...]
    ppermute x6, waiting for transfers between devices: 17.7 us -> 14.9 us  [padded_2(): after = lax.ppermute(first, axis, down)]
    ppermute x6, starting transfers between devices: 20.7 us -> 23.2 us  [padded_2(): before = lax.ppermute(last, axis, up)]
  transfers between devices with their start and end apart: 13 -> 16, of which waited for: 7 -> 9; matrix products, arithmetic and copies ran while one was open for 0% -> 1% of each run, Pallas kernels for 0% -> 0%
where the time goes in v1:
time: 129 us; the launch traced here: 128 us
  starting transfers between devices  37.1 us (29%)
  waiting for transfers between devices  37.1 us (29%)
  local copies, waits for them, and re-layouts  22.7 us (18%)
  between operations  14 us (11%)
  matrix products  9.77 us (8%)
  other arithmetic  7.33 us (6%)
    ppermute x6, starting transfers between devices, padded_2(): before = lax.ppermute(last, axis, up)  23.2 us
    reduce_scatter x1, waiting for transfers between devices, shards(): lax.psum_scatter((colour * jnp.exp(-front)).astype(jnp.bfloat16), 'depth'...  17.4 us
    ppermute x6, waiting for transfers between devices, padded_2(): after = lax.ppermute(first, axis, down)  14.9 us
    ppermute x6, starting transfers between devices, padded_2(): after = lax.ppermute(first, axis, down)  9.64 us
    reshape x1, local copies, waits for them, and re-layouts, shards(): brick_features.reshape(feat_count, windows, SAMPLES).transpose(1, 2, 0)  5.43 us
    dot_general x27, matrix products, convolve_valid(): jnp.dot(window, weights[tap], preferred_element_type=jnp.float32)  4.51 us
    ppermute x2, waiting for transfers between devices, collect(): from_left = lax.ppermute(from_left, axis, right)  4.32 us
    gather x2, local copies, waits for them, and re-layouts, march_block(): jnp.take(table, window_ids, axis=0)  3.91 us
  transfers between devices with their start and end apart: 16, of which 9 were waited for; matrix products, arithmetic and copies ran while one was open for 1% of the time, Pallas kernels for 0%

profile of v1, /device:TPU:1, one launch (start us, length us, event | category | flops | bytes accessed | tf_op | source)
XLA Modules:
  0.0 128.4 jit_solution(14020715099765495303)
XLA Ops:
  9.8 5.4 %reshape.274 = bf16[16,1024,16]{2,1,0:T(8,128)(2,1)} reshape(bf16[16,1,1,16384]{3,0,2,1:T(8,128)(2,1)} %param.13) | data formatting | bytes 1048576 | tf_op jit(solution)/shard_map/reshape | solution.py:92
  15.2 3.7 %copy.13 = bf16[1024,16,16]{0,2,1:T(8,128)(2,1)S(1)} copy(bf16[1024,16,16]{1,0,2:T(8,128)(2,1)} %bitcast.219) | data formatting | bytes 1048576 | tf_op jit(solution)/shard_map/transpose | solution.py:93
  19.1 19.6 %while.14 = (s32[]{:T(128)}, f32[2,32,512]{2,1,0:T(8,128)S(1)}, f32[2,512]{1,0:T(2,128)S(1)}, s32[2,512]{1,0:T(2,128)S(1)}, s32[2,512]{1,0:T(2,128)S(1)}, /*inde...) while((s32[]{:T(128)}, f32[2,32,512]{2,1,0:T(8,128)S(1)}, ...), condition=%wide.region_3.5_spmd, body=%wide.region_0.4_spmd.sunk | while | flops 110472448 | bytes 23171440 | solution.py:128
  19.2 2.0 %gather_fusion.1 = bf16[512,256]{1,0:T(8,128)(2,1)S(1)} fusion(bf16[1024,256]{1,0:T(8,128)(2,1)S(1)} %get-tuple-element.290, s32[1024]{0:T(1024)S(1)} %pad_clamp_fusion.5), kind=kCustom, calls=%fused_computation.clone.clone.1 | custom fusion | bytes 526336 | tf_op jit(solution)/shard_map/while/body/eval_jaxpr/jit(_take)/gather | solution.py:109
  21.4 2.0 %gather_fusion = bf16[512,256]{1,0:T(8,128)(2,1)S(1)} fusion(bf16[1024,256]{1,0:T(8,128)(2,1)S(1)} %get-tuple-element.290, s32[1024]{0:T(1024)S(1)} %pad_clamp_fusion.4), kind=kCustom, calls=%fused_computation.1.clone.clone.1 | custom fusion | bytes 526336 | tf_op jit(solution)/shard_map/while/body/eval_jaxpr/jit(_take)/gather | solution.py:109
  29.0 2.0 %gather_fusion.1 = bf16[512,256]{1,0:T(8,128)(2,1)S(1)} fusion(bf16[1024,256]{1,0:T(8,128)(2,1)S(1)} %get-tuple-element.290, s32[1024]{0:T(1024)S(1)} %pad_clamp_fusion.5), kind=kCustom, calls=%fused_computation.clone.clone.1 | custom fusion | bytes 526336 | tf_op jit(solution)/shard_map/while/body/eval_jaxpr/jit(_take)/gather | solution.py:109
  31.1 2.0 %gather_fusion = bf16[512,256]{1,0:T(8,128)(2,1)S(1)} fusion(bf16[1024,256]{1,0:T(8,128)(2,1)S(1)} %get-tuple-element.290, s32[1024]{0:T(1024)S(1)} %pad_clamp_fusion.4), kind=kCustom, calls=%fused_computation.1.clone.clone.1 | custom fusion | bytes 526336 | tf_op jit(solution)/shard_map/while/body/eval_jaxpr/jit(_take)/gather | solution.py:109
  38.7 2.2 %collective-permute-start = (f32[1,1024]{1,0:T(1,128)S(1)}, f32[1,1024]{1,0:T(1,128)S(1)}, u32[]{:S(2)}, u32[]{:S(2)}) collective-permute-start(f32[1,1024]{1,0:T(1,128)S(1)} %bitcast.261), channel_id=1, source_target_pairs={{0,4},{4,8},{8,12},{12,0},{1,5},{5,9},{9,13},{13,1},{2,6},{6,10},{... | collective-permute-start | bytes 12296 | tf_op jit(solution)/shard_map/ppermute | solution.py:21
  40.9 2.1 %collective-permute-start.1 = (f32[1,1024]{1,0:T(1,128)S(1)}, f32[1,1024]{1,0:T(1,128)S(1)}, u32[]{:S(2)}, u32[]{:S(2)}) collective-permute-start(f32[1,1024]{1,0:T(1,128)S(1)} %bitcast.262), channel_id=1, source_target_pairs={{0,12},{4,0},{8,4},{12,8},{1,13},{5,1},{9,5},{13,9},{2,14},{6,2},{... | collective-permute-start | bytes 12296 | tf_op jit(solution)/shard_map/ppermute | solution.py:26
  44.8 3.4 %collective-permute-done.2 = f32[1,1024]{1,0:T(1,128)S(1)} collective-permute-done((f32[1,1024]{1,0:T(1,128)S(1)}, f32[1,1024]{1,0:T(1,128)S(1)}, u32[]{:S(2)}, u32[]{:S(2)}) %collective-permute-start.2) | collective-permute-done | bytes 4128 | tf_op jit(solution)/shard_map/ppermute | solution.py:21
  49.7 17.4 %reduce-scatter.2.cloned.1.call-done = bf16[32,256]{1,0:T(8,128)(2,1)} async-done(((bf16[32,1024]{1,0:T(8,128)(2,1)}), bf16[32,256]{1,0:T(8,128)(2,1)}) %reduce-scatter.2.cloned.1.call-update) | async-done | bytes 16400 | tf_op jit(solution)/shard_map/reduce_scatter | solution.py:137
  70.5 3.0 %collective-permute-done.4 = bf16[1,16,32]{2,1,0:T(8,128)(2,1)S(1)} collective-permute-done((bf16[1,16,32]{2,1,0:T(8,128)(2,1)S(1)}, bf16[1,16,32]{2,1,0:T(8,128)(2,1)S(1)}, u32[]{:S(2)}, u32[]{:S(2)}) %collective-permute-start.4) | collective-permute-done | bytes 1056 | tf_op jit(solution)/shard_map/ppermute | solution.py:41
  73.6 7.1 %collective-permute-start.5 = (bf16[18,1,32]{2,1,0:T(2,128)(2,1)S(1)}, bf16[18,1,32]{2,1,0:T(2,128)(2,1)S(1)}, u32[]{:S(2)}, u32[]{:S(2)}) collective-permute-start(bf16[18,1,32]{2,1,0:T(2,128)(2,1)S(1)} %get-tuple-element.175), channel_id=1, source_target_pairs={{0,1},{1,2},{2,3},{4,5},{5,6},{6,7},{8,9},{9,10},{10,11},{12,13},{... | collective-permute-start | bytes 3464 | tf_op jit(solution)/shard_map/ppermute | solution.py:40
  80.7 1.9 %collective-permute-start.6 = (bf16[18,1,32]{2,1,0:T(2,128)(2,1)S(1)}, bf16[18,1,32]{2,1,0:T(2,128)(2,1)S(1)}, u32[]{:S(2)}, u32[]{:S(2)}) collective-permute-start(bf16[18,1,32]{2,1,0:T(2,128)(2,1)S(1)} %get-tuple-element.176), channel_id=1, source_target_pairs={{1,0},{2,1},{3,2},{5,4},{6,5},{7,6},{9,8},{10,9},{11,10},{13,12},{... | collective-permute-start | bytes 3464 | tf_op jit(solution)/shard_map/ppermute | solution.py:41
  82.8 2.9 %collective-permute-done.6 = bf16[18,1,32]{2,1,0:T(2,128)(2,1)S(1)} collective-permute-done((bf16[18,1,32]{2,1,0:T(2,128)(2,1)S(1)}, bf16[18,1,32]{2,1,0:T(2,128)(2,1)S(1)}, u32[]{:S(2)}, u32[]{:S(2)}) %collective-permute-start.6) | collective-permute-done | bytes 1184 | tf_op jit(solution)/shard_map/ppermute | solution.py:41
  86.9 3.4 %collective-permute-start.7 = (bf16[1,16,128]{2,1,0:T(8,128)(2,1)S(1)}, bf16[1,16,128]{2,1,0:T(8,128)(2,1)S(1)}, u32[]{:S(2)}, u32[]{:S(2)}) collective-permute-start(bf16[1,16,128]{2,1,0:T(8,128)(2,1)S(1)} %get-tuple-element.183), channel_id=1, source_target_pairs={{0,4},{4,8},{8,12},{1,5},{5,9},{9,13},{2,6},{6,10},{10,14},{3,7},{... | collective-permute-start | bytes 12296 | tf_op jit(solution)/shard_map/ppermute | solution.py:40
  91.7 3.0 %collective-permute-done.8 = bf16[1,16,128]{2,1,0:T(8,128)(2,1)S(1)} collective-permute-done((bf16[1,16,128]{2,1,0:T(8,128)(2,1)S(1)}, bf16[1,16,128]{2,1,0:T(8,128)(2,1)S(1)}, u32[]{:S(2)}, u32[]{:S(2)}) %collective-permute-start.8) | collective-permute-done | bytes 4128 | tf_op jit(solution)/shard_map/ppermute | solution.py:41
  94.7 1.9 %collective-permute-start.10 = (bf16[18,1,128]{2,1,0:T(2,128)(2,1)S(1)}, bf16[18,1,128]{2,1,0:T(2,128)(2,1)S(1)}, u32[]{:S(2)}, u32[]{:S(2)}) collective-permute-start(bf16[18,1,128]{2,1,0:T(2,128)(2,1)S(1)} %get-tuple-element.172), channel_id=1, source_target_pairs={{1,0},{2,1},{3,2},{5,4},{6,5},{7,6},{9,8},{10,9},{11,10},{13,12},{... | collective-permute-start | bytes 13832 | tf_op jit(solution)/shard_map/ppermute | solution.py:41
  96.6 3.6 %collective-permute-start.9 = (bf16[18,1,128]{2,1,0:T(2,128)(2,1)S(1)}, bf16[18,1,128]{2,1,0:T(2,128)(2,1)S(1)}, u32[]{:S(2)}, u32[]{:S(2)}) collective-permute-start(bf16[18,1,128]{2,1,0:T(2,128)(2,1)S(1)} %get-tuple-element.171), channel_id=1, source_target_pairs={{0,1},{1,2},{2,3},{4,5},{5,6},{6,7},{8,9},{9,10},{10,11},{12,13},{... | collective-permute-start | bytes 13832 | tf_op jit(solution)/shard_map/ppermute | solution.py:40
  102.4 2.1 %collective-permute-start.11 = (bf16[1,16,128]{2,1,0:T(8,128)(2,1)S(1)}, bf16[1,16,128]{2,1,0:T(8,128)(2,1)S(1)}, u32[]{:S(2)}, u32[]{:S(2)}) collective-permute-start(bf16[1,16,128]{2,1,0:T(8,128)(2,1)S(1)} %get-tuple-element.179), channel_id=1, source_target_pairs={{0,4},{4,8},{8,12},{1,5},{5,9},{9,13},{2,6},{6,10},{10,14},{3,7},{... | collective-permute-start | bytes 12296 | tf_op jit(solution)/shard_map/ppermute | solution.py:40
  105.9 3.0 %collective-permute-done.12 = bf16[1,16,128]{2,1,0:T(8,128)(2,1)S(1)} collective-permute-done((bf16[1,16,128]{2,1,0:T(8,128)(2,1)S(1)}, bf16[1,16,128]{2,1,0:T(8,128)(2,1)S(1)}, u32[]{:S(2)}, u32[]{:S(2)}) %collective-permute-start.12) | collective-permute-done | bytes 4128 | tf_op jit(solution)/shard_map/ppermute | solution.py:41
  108.9 5.6 %collective-permute-start.13 = (bf16[18,1,128]{2,1,0:T(2,128)(2,1)S(1)}, bf16[18,1,128]{2,1,0:T(2,128)(2,1)S(1)}, u32[]{:S(2)}, u32[]{:S(2)}) collective-permute-start(bf16[18,1,128]{2,1,0:T(2,128)(2,1)S(1)} %get-tuple-element.167), channel_id=1, source_target_pairs={{0,1},{1,2},{2,3},{4,5},{5,6},{6,7},{8,9},{9,10},{10,11},{12,13},{... | collective-permute-start | bytes 13832 | tf_op jit(solution)/shard_map/ppermute | solution.py:40
  114.6 1.9 %collective-permute-start.14 = (bf16[18,1,128]{2,1,0:T(2,128)(2,1)S(1)}, bf16[18,1,128]{2,1,0:T(2,128)(2,1)S(1)}, u32[]{:S(2)}, u32[]{:S(2)}) collective-permute-start(bf16[18,1,128]{2,1,0:T(2,128)(2,1)S(1)} %get-tuple-element.168), channel_id=1, source_target_pairs={{1,0},{2,1},{3,2},{5,4},{6,5},{7,6},{9,8},{10,9},{11,10},{13,12},{... | collective-permute-start | bytes 13832 | tf_op jit(solution)/shard_map/ppermute | solution.py:41
  116.7 2.9 %collective-permute-done.14 = bf16[18,1,128]{2,1,0:T(2,128)(2,1)S(1)} collective-permute-done((bf16[18,1,128]{2,1,0:T(2,128)(2,1)S(1)}, bf16[18,1,128]{2,1,0:T(2,128)(2,1)S(1)}, u32[]{:S(2)}, u32[]{:S(2)}) %collective-permute-start.14) | collective-permute-done | bytes 4640 | tf_op jit(solution)/shard_map/ppermute | solution.py:41
  (150 shorter events, 29.6 us)
Async XLA Ops:
  6.5 60.5 %reduce-scatter.2.cloned.1.call-start = ((), (), s32[]{:S(2)}) async-start(), calls=%async_computation.1 | async-start | bytes 81920 | tf_op jit(solution)/shard_map/reduce_scatter | solution.py:137
  15.2 3.9 %copy-start.2 = (bf16[128,33]{0,1:T(8,128)(2,1)S(1)}, bf16[128,33]{0,1:T(8,128)(2,1)}, u32[]{:S(2)}) copy-start(bf16[128,33]{0,1:T(8,128)(2,1)} %param.18) | copy-start | bytes 25348
  15.2 3.9 %copy-start.3 = (bf16[16,128]{1,0:T(8,128)(2,1)S(1)}, bf16[16,128]{1,0:T(8,128)(2,1)}, u32[]{:S(2)}) copy-start(bf16[16,128]{1,0:T(8,128)(2,1)} %param.17) | copy-start | bytes 12292
  19.1 24.9 %copy-start.5 = (s32[1,4]{1,0:T(1,128)S(1)}, s32[1,4]{1,0:T(1,128)}, u32[]{:S(2)}) copy-start(s32[1,4]{1,0:T(1,128)} %param.16) | copy-start | bytes 52
  19.1 63.5 %copy-start.4 = (bf16[9,32,128]{2,1,0:T(8,128)(2,1)S(1)}, bf16[9,32,128]{2,1,0:T(8,128)(2,1)}, u32[]{:S(2)}) copy-start(bf16[9,32,128]{2,1,0:T(8,128)(2,1)} %param.19) | copy-start | bytes 221188
  38.7 5.2 %collective-permute-start = (f32[1,1024]{1,0:T(1,128)S(1)}, f32[1,1024]{1,0:T(1,128)S(1)}, u32[]{:S(2)}, u32[]{:S(2)}) collective-permute-start(f32[1,1024]{1,0:T(1,128)S(1)} %bitcast.261), channel_id=1, source_target_pairs={{0,4},{4,8},{8,12},{12,0},{1,5},{5,9},{9,13},{13,1},{2,6},{6,10},{... | collective-permute-start | bytes 12296 | tf_op jit(solution)/shard_map/ppermute | solution.py:21
  40.9 3.8 %collective-permute-start.1 = (f32[1,1024]{1,0:T(1,128)S(1)}, f32[1,1024]{1,0:T(1,128)S(1)}, u32[]{:S(2)}, u32[]{:S(2)}) collective-permute-start(f32[1,1024]{1,0:T(1,128)S(1)} %bitcast.262), channel_id=1, source_target_pairs={{0,12},{4,0},{8,4},{12,8},{1,13},{5,1},{9,5},{13,9},{2,14},{6,2},{... | collective-permute-start | bytes 12296 | tf_op jit(solution)/shard_map/ppermute | solution.py:26
  43.9 4.3 %collective-permute-start.2 = (f32[1,1024]{1,0:T(1,128)S(1)}, f32[1,1024]{1,0:T(1,128)S(1)}, u32[]{:S(2)}, u32[]{:S(2)}) collective-permute-start(f32[1,1024]{1,0:T(1,128)S(1)} %collective-permute-done), channel_id=1, source_target_pairs={{0,4},{4,8},{8,12},{12,0},{1,5},{5,9},{9,13},{13,1},{2,6},{6,10},{... | collective-permute-start | bytes 12296 | tf_op jit(solution)/shard_map/ppermute | solution.py:21
  67.9 2.6 %collective-permute-start.3 = (bf16[1,16,32]{2,1,0:T(8,128)(2,1)S(1)}, bf16[1,16,32]{2,1,0:T(8,128)(2,1)S(1)}, u32[]{:S(2)}, u32[]{:S(2)}) collective-permute-start(bf16[1,16,32]{2,1,0:T(8,128)(2,1)S(1)} %get-tuple-element.187), channel_id=1, source_target_pairs={{0,4},{4,8},{8,12},{1,5},{5,9},{9,13},{2,6},{6,10},{10,14},{3,7},{... | collective-permute-start | bytes 3080 | tf_op jit(solution)/shard_map/ppermute | solution.py:40
  69.2 4.4 %collective-permute-start.4 = (bf16[1,16,32]{2,1,0:T(8,128)(2,1)S(1)}, bf16[1,16,32]{2,1,0:T(8,128)(2,1)S(1)}, u32[]{:S(2)}, u32[]{:S(2)}) collective-permute-start(bf16[1,16,32]{2,1,0:T(8,128)(2,1)S(1)} %get-tuple-element.188), channel_id=1, source_target_pairs={{4,0},{8,4},{12,8},{5,1},{9,5},{13,9},{6,2},{10,6},{14,10},{7,3},{... | collective-permute-start | bytes 3080 | tf_op jit(solution)/shard_map/ppermute | solution.py:41
  73.6 9.2 %collective-permute-start.5 = (bf16[18,1,32]{2,1,0:T(2,128)(2,1)S(1)}, bf16[18,1,32]{2,1,0:T(2,128)(2,1)S(1)}, u32[]{:S(2)}, u32[]{:S(2)}) collective-permute-start(bf16[18,1,32]{2,1,0:T(2,128)(2,1)S(1)} %get-tuple-element.175), channel_id=1, source_target_pairs={{0,1},{1,2},{2,3},{4,5},{5,6},{6,7},{8,9},{9,10},{10,11},{12,13},{... | collective-permute-start | bytes 3464 | tf_op jit(solution)/shard_map/ppermute | solution.py:40
  80.7 5.0 %collective-permute-start.6 = (bf16[18,1,32]{2,1,0:T(2,128)(2,1)S(1)}, bf16[18,1,32]{2,1,0:T(2,128)(2,1)S(1)}, u32[]{:S(2)}, u32[]{:S(2)}) collective-permute-start(bf16[18,1,32]{2,1,0:T(2,128)(2,1)S(1)} %get-tuple-element.176), channel_id=1, source_target_pairs={{1,0},{2,1},{3,2},{5,4},{6,5},{7,6},{9,8},{10,9},{11,10},{13,12},{... | collective-permute-start | bytes 3464 | tf_op jit(solution)/shard_map/ppermute | solution.py:41
  82.7 17.7 %copy-start = (bf16[9,128,128]{2,1,0:T(8,128)(2,1)S(1)}, bf16[9,128,128]{2,1,0:T(8,128)(2,1)}, u32[]{:S(2)}) copy-start(bf16[9,128,128]{2,1,0:T(8,128)(2,1)} %param.20) | copy-start | bytes 884740
  86.9 4.7 %collective-permute-start.7 = (bf16[1,16,128]{2,1,0:T(8,128)(2,1)S(1)}, bf16[1,16,128]{2,1,0:T(8,128)(2,1)S(1)}, u32[]{:S(2)}, u32[]{:S(2)}) collective-permute-start(bf16[1,16,128]{2,1,0:T(8,128)(2,1)S(1)} %get-tuple-element.183), channel_id=1, source_target_pairs={{0,4},{4,8},{8,12},{1,5},{5,9},{9,13},{2,6},{6,10},{10,14},{3,7},{... | collective-permute-start | bytes 12296 | tf_op jit(solution)/shard_map/ppermute | solution.py:40
  90.3 4.4 %collective-permute-start.8 = (bf16[1,16,128]{2,1,0:T(8,128)(2,1)S(1)}, bf16[1,16,128]{2,1,0:T(8,128)(2,1)S(1)}, u32[]{:S(2)}, u32[]{:S(2)}) collective-permute-start(bf16[1,16,128]{2,1,0:T(8,128)(2,1)S(1)} %get-tuple-element.184), channel_id=1, source_target_pairs={{4,0},{8,4},{12,8},{5,1},{9,5},{13,9},{6,2},{10,6},{14,10},{7,3},{... | collective-permute-start | bytes 12296 | tf_op jit(solution)/shard_map/ppermute | solution.py:41
  94.7 5.8 %collective-permute-start.10 = (bf16[18,1,128]{2,1,0:T(2,128)(2,1)S(1)}, bf16[18,1,128]{2,1,0:T(2,128)(2,1)S(1)}, u32[]{:S(2)}, u32[]{:S(2)}) collective-permute-start(bf16[18,1,128]{2,1,0:T(2,128)(2,1)S(1)} %get-tuple-element.172), channel_id=1, source_target_pairs={{1,0},{2,1},{3,2},{5,4},{6,5},{7,6},{9,8},{10,9},{11,10},{13,12},{... | collective-permute-start | bytes 13832 | tf_op jit(solution)/shard_map/ppermute | solution.py:41
  96.6 4.4 %collective-permute-start.9 = (bf16[18,1,128]{2,1,0:T(2,128)(2,1)S(1)}, bf16[18,1,128]{2,1,0:T(2,128)(2,1)S(1)}, u32[]{:S(2)}, u32[]{:S(2)}) collective-permute-start(bf16[18,1,128]{2,1,0:T(2,128)(2,1)S(1)} %get-tuple-element.171), channel_id=1, source_target_pairs={{0,1},{1,2},{2,3},{4,5},{5,6},{6,7},{8,9},{9,10},{10,11},{12,13},{... | collective-permute-start | bytes 13832 | tf_op jit(solution)/shard_map/ppermute | solution.py:40
  100.5 16.0 %copy-start.1 = (bf16[9,128,128]{2,1,0:T(8,128)(2,1)S(1)}, bf16[9,128,128]{2,1,0:T(8,128)(2,1)}, u32[]{:S(2)}) copy-start(bf16[9,128,128]{2,1,0:T(8,128)(2,1)} %param.21) | copy-start | bytes 884740
  102.4 3.4 %collective-permute-start.11 = (bf16[1,16,128]{2,1,0:T(8,128)(2,1)S(1)}, bf16[1,16,128]{2,1,0:T(8,128)(2,1)S(1)}, u32[]{:S(2)}, u32[]{:S(2)}) collective-permute-start(bf16[1,16,128]{2,1,0:T(8,128)(2,1)S(1)} %get-tuple-element.179), channel_id=1, source_target_pairs={{0,4},{4,8},{8,12},{1,5},{5,9},{9,13},{2,6},{6,10},{10,14},{3,7},{... | collective-permute-start | bytes 12296 | tf_op jit(solution)/shard_map/ppermute | solution.py:40
  104.6 4.4 %collective-permute-start.12 = (bf16[1,16,128]{2,1,0:T(8,128)(2,1)S(1)}, bf16[1,16,128]{2,1,0:T(8,128)(2,1)S(1)}, u32[]{:S(2)}, u32[]{:S(2)}) collective-permute-start(bf16[1,16,128]{2,1,0:T(8,128)(2,1)S(1)} %get-tuple-element.180), channel_id=1, source_target_pairs={{4,0},{8,4},{12,8},{5,1},{9,5},{13,9},{6,2},{10,6},{14,10},{7,3},{... | collective-permute-start | bytes 12296 | tf_op jit(solution)/shard_map/ppermute | solution.py:41
  108.9 7.7 %collective-permute-start.13 = (bf16[18,1,128]{2,1,0:T(2,128)(2,1)S(1)}, bf16[18,1,128]{2,1,0:T(2,128)(2,1)S(1)}, u32[]{:S(2)}, u32[]{:S(2)}) collective-permute-start(bf16[18,1,128]{2,1,0:T(2,128)(2,1)S(1)} %get-tuple-element.167), channel_id=1, source_target_pairs={{0,1},{1,2},{2,3},{4,5},{5,6},{6,7},{8,9},{9,10},{10,11},{12,13},{... | collective-permute-start | bytes 13832 | tf_op jit(solution)/shard_map/ppermute | solution.py:40
  114.6 5.0 %collective-permute-start.14 = (bf16[18,1,128]{2,1,0:T(2,128)(2,1)S(1)}, bf16[18,1,128]{2,1,0:T(2,128)(2,1)S(1)}, u32[]{:S(2)}, u32[]{:S(2)}) collective-permute-start(bf16[18,1,128]{2,1,0:T(2,128)(2,1)S(1)} %get-tuple-element.168), channel_id=1, source_target_pairs={{1,0},{2,1},{3,2},{5,4},{6,5},{7,6},{9,8},{10,9},{11,10},{13,12},{... | collective-permute-start | bytes 13832 | tf_op jit(solution)/shard_map/ppermute | solution.py:41
Sparse Core Ops, SparseCore 0:
  49.8 17.1 reduce-scatter.1
